TPU v7x, 512 devices: a whole 4x4x16 slice. The times are simulated.
512 devices in a mesh: row: 64 (over x, z), col: 8 (over y, core).
Axes of the slice: x: 4, y: 4, z: 16, core: 2. Of those that a mesh axis runs over, the one named last changes fastest.
Arguments:
- panel: float32 [512, 131072], P('col', 'row'), may hold values from -6 to 6
- signs: int32 [131072], P('row'), may hold values from -1 to 1, as said below
- sample_rows: int32 [8192], P('row'), may hold values from 0 to 131071, as said below
Outputs:
- sketch: float32 [512, 8192], P('col', 'row')
- gram: float32 [512, 512], P('row')
Inputs may be any that keep to these rules, and one draw needn't show every extreme that they name: `sample_rows`: sorted ascending and distinct; entries b * 128 to (b + 1) * 128 - 1 lie in rows b * 2048 to (b + 1) * 2048 - 1. `signs`: each entry is -1 or 1.
All inputs are finite; a program needn't handle non-finite values.
Results may differ from a plain program's by a relative error of at most 0.00013.
Values sent between devices are 32-bit elements; how exact they have to be, the bound alone decides.
A program may use at most 64 MiB of HBM per device.

v0:
```python
import jax
import jax.numpy as jnp
from jax import lax
from jax.sharding import PartitionSpec as P


def partner(value, axis, stride):
    mask = 2**stride
    pairs = [(source, source ^ mask) for source in range(lax.axis_size(axis))]
    return lax.ppermute(value, axis, pairs)


def hadamard_table(order):
    first = jnp.arange(order, dtype=jnp.int32)[:, None]
    second = jnp.arange(order, dtype=jnp.int32)[None, :]
    parity = jnp.zeros((order, order), jnp.int32)
    for level in range(order.bit_length() - 1):
        parity = parity + jnp.bitwise_and(jnp.right_shift(first, level), 1) * jnp.bitwise_and(
            jnp.right_shift(second, level), 1
        )
    return (1 - 2 * (parity % 2)).astype(jnp.float32)


def per_device(panel, signs, sample_rows):
    high = lax.Precision.HIGHEST
    width, length = panel.shape
    groups = lax.axis_size("row")
    mine = lax.axis_index("row")
    total_rows = length * groups
    signed = panel * signs[None, :].astype(jnp.float32)
    shaped = signed.reshape(width, length // 128, 128)
    shaped = jnp.einsum("cab,be->cae", shaped, hadamard_table(128), precision=high)
    shaped = jnp.einsum("fa,cab->cfb", hadamard_table(length // 128), shaped, precision=high)
    local_mix = shaped.reshape(width, length)
    held = local_mix
    for level in range(groups.bit_length() - 1):
        other = partner(held, "row", level)
        upper = jnp.bitwise_and(jnp.right_shift(mine, level), 1) == 1
        held = jnp.where(upper, other - held, held + other)
    held = held / jnp.sqrt(jnp.float32(total_rows))
    place = sample_rows - mine * length
    sketch = jnp.take(held, place, axis=1)
    per_dev = sketch.shape[1]
    full_cols = lax.all_gather(sketch, "col", axis=0, tiled=True)
    samples_all = per_dev * groups
    my_block = lax.psum_scatter(
        jnp.dot(full_cols, sketch.T, precision=high, preferred_element_type=jnp.float32)
        / samples_all,
        "row",
        scatter_dimension=0,
        tiled=True,
    )
    gram = lax.all_gather(my_block, "col", axis=1, tiled=True)
    return (sketch, gram)


def solution(mesh):
    return jax.shard_map(
        per_device,
        mesh=mesh,
        in_specs=(P("col", "row"), P("row"), P("row")),
        out_specs=(P("col", "row"), P("row", None)),
        check_vma=False,
    )
```

profile of v0, /device:TPU:1, one launch (start us, length us, event | category | flops | bytes accessed | tf_op | source)
XLA Modules:
  0.0 496.7 jit_solution(11359555812915848403)
XLA Ops:
  7.3 0.6 copy-done.1
  7.9 1.1 multiply_bitcast_fusion
  9.1 0.7 fusion.5
  9.8 0.6 fusion.35
  10.6 4.4 collective-permute-start
  15.0 0.3 copy.15
  15.3 6.7 %collective-permute-done = f32[64,2048]{1,0:T(8,128)S(1)} collective-permute-done((f32[64,2048]{1,0:T(8,128)S(1)}, f32[64,2048]{1,0:T(8,128)S(1)}, u32[]{:S(2)}, u32[]{:S(2)}) %collective-permute-start) | collective-permute-done | bytes 524320 | tf_op jit(solution)/shard_map/ppermute | solution.py:10
  22.0 0.3 copy.14
  22.8 9.4 %collective-permute-start.1 = (f32[64,2048]{1,0:T(8,128)S(1)}, f32[64,2048]{1,0:T(8,128)S(1)}, u32[]{:S(2)}, u32[]{:S(2)}) collective-permute-start(f32[64,2048]{1,0:T(8,128)S(1)} %copy.18), channel_id=1, source_target_pairs={{0,16},{8,24},{16,0},{24,8},{32,48},{40,56},{48,32},{56,40},{64,80... | collective-permute-start | bytes 1572872 | tf_op jit(solution)/shard_map/ppermute | solution.py:10
  32.2 22.6 %collective-permute-done.1 = f32[64,2048]{1,0:T(8,128)S(1)} collective-permute-done((f32[64,2048]{1,0:T(8,128)S(1)}, f32[64,2048]{1,0:T(8,128)S(1)}, u32[]{:S(2)}, u32[]{:S(2)}) %collective-permute-start.1) | collective-permute-done | bytes 524320 | tf_op jit(solution)/shard_map/ppermute | solution.py:10
  54.8 0.3 copy.19
  55.6 8.8 %collective-permute-start.2 = (f32[64,2048]{1,0:T(8,128)S(1)}, f32[64,2048]{1,0:T(8,128)S(1)}, u32[]{:S(2)}, u32[]{:S(2)}) collective-permute-start(f32[64,2048]{1,0:T(8,128)S(1)} %copy.21), channel_id=1, source_target_pairs={{0,32},{8,40},{16,48},{24,56},{32,0},{40,8},{48,16},{56,24},{64,96... | collective-permute-start | bytes 1572872 | tf_op jit(solution)/shard_map/ppermute | solution.py:10
  64.4 45.1 %collective-permute-done.2 = f32[64,2048]{1,0:T(8,128)S(1)} collective-permute-done((f32[64,2048]{1,0:T(8,128)S(1)}, f32[64,2048]{1,0:T(8,128)S(1)}, u32[]{:S(2)}, u32[]{:S(2)}) %collective-permute-start.2) | collective-permute-done | bytes 524320 | tf_op jit(solution)/shard_map/ppermute | solution.py:10
  109.4 0.3 copy.22
  110.2 24.3 %collective-permute-start.3 = (f32[64,2048]{1,0:T(8,128)S(1)}, f32[64,2048]{1,0:T(8,128)S(1)}, u32[]{:S(2)}, u32[]{:S(2)}) collective-permute-start(f32[64,2048]{1,0:T(8,128)S(1)} %copy.24), channel_id=1, source_target_pairs={{0,64},{8,72},{16,80},{24,88},{32,96},{40,104},{48,112},{56,120},{... | collective-permute-start | bytes 1572872 | tf_op jit(solution)/shard_map/ppermute | solution.py:10
  134.5 16.9 %collective-permute-done.3 = f32[64,2048]{1,0:T(8,128)S(1)} collective-permute-done((f32[64,2048]{1,0:T(8,128)S(1)}, f32[64,2048]{1,0:T(8,128)S(1)}, u32[]{:S(2)}, u32[]{:S(2)}) %collective-permute-start.3) | collective-permute-done | bytes 524320 | tf_op jit(solution)/shard_map/ppermute | solution.py:10
  151.4 0.3 copy.25
  152.2 3.1 collective-permute-start.4
  155.3 11.7 %collective-permute-done.4 = f32[64,2048]{1,0:T(8,128)S(1)} collective-permute-done((f32[64,2048]{1,0:T(8,128)S(1)}, f32[64,2048]{1,0:T(8,128)S(1)}, u32[]{:S(2)}, u32[]{:S(2)}) %collective-permute-start.4) | collective-permute-done | bytes 524320 | tf_op jit(solution)/shard_map/ppermute | solution.py:10
  167.1 0.3 copy.28
  167.8 4.6 collective-permute-start.5
  172.5 0.6 copy-done.2
  173.2 10.1 %collective-permute-done.5 = f32[64,2048]{1,0:T(8,128)S(1)} collective-permute-done((f32[64,2048]{1,0:T(8,128)S(1)}, f32[64,2048]{1,0:T(8,128)S(1)}, u32[]{:S(2)}, u32[]{:S(2)}) %collective-permute-start.5) | collective-permute-done | bytes 524320 | tf_op jit(solution)/shard_map/ppermute | solution.py:10
  183.3 0.3 copy.31
  183.8 0.6 gather_fusion
  184.6 15.4 %all_gather.6 = f32[512,128]{1,0:T(8,128)S(1)} all-gather(f32[64,128]{1,0:T(8,128)S(1)} %copy.35), channel_id=1, replica_groups=mesh['row'=64,'col'=8] {'col'}, dimensions={0}, use_global_device_ids=true | all-gather | bytes 294912 | tf_op jit(solution)/shard_map/all_gather | solution.py:44
  200.1 1.1 convolution_multiply_fusion
  201.2 1.3 dynamic-slice
  203.1 261.8 %all-reduce.3.cloned.1.call-done = f32[512,64]{1,0:T(8,128)} async-done(((f32[512,64]{1,0:T(8,128)}), f32[512,64]{1,0:T(8,128)}) %all-reduce.3.cloned.1.call-update) | async-done | bytes 131088
  465.0 0.7 dynamic-slice_bitcast_fusion
  465.7 23.5 %all-gather = f32[8,64,8]{1,2,0:T(8,128)S(1)} all-gather(f32[1,64,8]{1,2,0:T(8,128)S(1)} %dynamic-slice_bitcast_fusion), channel_id=1, replica_groups=mesh['row'=64,'col'=8] {'col'}, dimensions={0}, use_global_device_ids=true | all-gather | bytes 18432 | tf_op jit(solution)/shard_map/all_gather | solution.py:53
  489.2 0.7 reshape.183
  (31 shorter events, 2.8 us)
Async XLA Ops:
  7.2 0.7 copy-start.1
  7.2 457.8 %all-reduce.3.cloned.1.call-start = ((), (), s32[]{:S(2)}) async-start(), calls=%async_computation | async-start | bytes 524288
  10.6 11.4 %collective-permute-start = (f32[64,2048]{1,0:T(8,128)S(1)}, f32[64,2048]{1,0:T(8,128)S(1)}, u32[]{:S(2)}, u32[]{:S(2)}) collective-permute-start(f32[64,2048]{1,0:T(8,128)S(1)} %bitcast.27), channel_id=1, source_target_pairs={{0,8},{8,0},{16,24},{24,16},{32,40},{40,32},{48,56},{56,48},{64,72... | collective-permute-start | bytes 1572872 | tf_op jit(solution)/shard_map/ppermute | solution.py:10
  22.8 32.0 %collective-permute-start.1 = (f32[64,2048]{1,0:T(8,128)S(1)}, f32[64,2048]{1,0:T(8,128)S(1)}, u32[]{:S(2)}, u32[]{:S(2)}) collective-permute-start(f32[64,2048]{1,0:T(8,128)S(1)} %copy.18), channel_id=1, source_target_pairs={{0,16},{8,24},{16,0},{24,8},{32,48},{40,56},{48,32},{56,40},{64,80... | collective-permute-start | bytes 1572872 | tf_op jit(solution)/shard_map/ppermute | solution.py:10
  55.6 53.9 %collective-permute-start.2 = (f32[64,2048]{1,0:T(8,128)S(1)}, f32[64,2048]{1,0:T(8,128)S(1)}, u32[]{:S(2)}, u32[]{:S(2)}) collective-permute-start(f32[64,2048]{1,0:T(8,128)S(1)} %copy.21), channel_id=1, source_target_pairs={{0,32},{8,40},{16,48},{24,56},{32,0},{40,8},{48,16},{56,24},{64,96... | collective-permute-start | bytes 1572872 | tf_op jit(solution)/shard_map/ppermute | solution.py:10
  110.2 41.2 %collective-permute-start.3 = (f32[64,2048]{1,0:T(8,128)S(1)}, f32[64,2048]{1,0:T(8,128)S(1)}, u32[]{:S(2)}, u32[]{:S(2)}) collective-permute-start(f32[64,2048]{1,0:T(8,128)S(1)} %copy.24), channel_id=1, source_target_pairs={{0,64},{8,72},{16,80},{24,88},{32,96},{40,104},{48,112},{56,120},{... | collective-permute-start | bytes 1572872 | tf_op jit(solution)/shard_map/ppermute | solution.py:10
  152.2 14.9 %collective-permute-start.4 = (f32[64,2048]{1,0:T(8,128)S(1)}, f32[64,2048]{1,0:T(8,128)S(1)}, u32[]{:S(2)}, u32[]{:S(2)}) collective-permute-start(f32[64,2048]{1,0:T(8,128)S(1)} %copy.27), channel_id=1, source_target_pairs={{0,128},{8,136},{16,144},{24,152},{32,160},{40,168},{48,176},{56,1... | collective-permute-start | bytes 1572872 | tf_op jit(solution)/shard_map/ppermute | solution.py:10
  167.8 15.5 %collective-permute-start.5 = (f32[64,2048]{1,0:T(8,128)S(1)}, f32[64,2048]{1,0:T(8,128)S(1)}, u32[]{:S(2)}, u32[]{:S(2)}) collective-permute-start(f32[64,2048]{1,0:T(8,128)S(1)} %copy.30), channel_id=1, source_target_pairs={{0,256},{8,264},{16,272},{24,280},{32,288},{40,296},{48,304},{56,3... | collective-permute-start | bytes 1572872 | tf_op jit(solution)/shard_map/ppermute | solution.py:10
  172.5 0.7 copy-start.2
  184.6 15.5 %copy-start = (f32[64,128]{1,0:T(8,128)}, f32[64,128]{1,0:T(8,128)S(1)}, u32[]{:S(2)}) copy-start(f32[64,128]{1,0:T(8,128)S(1)} %copy.35) | copy-start | bytes 98308
Sparse Core Ops, SparseCore 0:
  201.3 263.5 all-reduce.2
where the time goes:
time: 497 us
  waiting for transfers between devices  375 us (75%)
  starting transfers between devices  54.7 us (11%)
  blocking collectives  38.9 us (8%)
  between operations  15 us (3%)
  local copies, waits for them, and re-layouts  8.7 us (2%)
    unnamed x2, waiting for transfers between devices  262 us
    ppermute x6, waiting for transfers between devices, partner(): return lax.ppermute(value, axis, pairs)  113 us
    ppermute x6, starting transfers between devices, partner(): return lax.ppermute(value, axis, pairs)  54.6 us
    all_gather x1, blocking collectives, per_device(): gram = lax.all_gather(my_block, 'col', axis=1, tiled=True)  23.5 us
    all_gather x1, blocking collectives, per_device(): full_cols = lax.all_gather(sketch, 'col', axis=0, tiled=True)  15.4 us
  transfers between devices with their start and end apart: 7, of which 7 were waited for; matrix products, arithmetic and copies ran while one was open for 0% of the time, Pallas kernels for 0%

commit v1 on v0

v1 whole, which is shorter than its diff:
```python
import functools

import jax
import jax.numpy as jnp
from jax import lax
from jax.experimental import pallas as pl
from jax.experimental.pallas import tpu as pltpu
from jax.sharding import PartitionSpec as P

MESH = pl.DeviceIdType.MESH
LANES = 128


def parity_sign(bits):
    bits = bits ^ (bits >> 4)
    bits = bits ^ (bits >> 2)
    bits = bits ^ (bits >> 1)
    return (1 - 2 * (bits & 1)).astype(jnp.float32)


def split_hi_lo(value):
    hi = value.astype(jnp.bfloat16)
    return hi, (value - hi.astype(jnp.float32)).astype(jnp.bfloat16)


def butterfly(blocks):
    blocks = list(blocks)
    step = 1
    while step < len(blocks):
        for first in range(len(blocks)):
            if not first & step:
                low, high = blocks[first], blocks[first + step]
                blocks[first], blocks[first + step] = low + high, low - high
        step *= 2
    return blocks


def kernel(
    dims, panel_ref, signs_ref, samp_ref, sketch_ref, gram_ref,
    panel, xs, xr, samples, had, mask, mixed, send_dn, send_up, recv_dn, recv_up,
    own, rows, tile, tile_in, final,
    panel_sem, sx_send, sx_recv, sz_send, sz_recv, x_send, x_recv,
    dn_send, dn_recv, up_send, up_recv, own_send, own_recv, row_send, row_recv,
    gz_send, gz_recv, gc_send, gc_recv,
):
    nx, nz, ny, nc, parts = dims
    width, length = panel.shape
    block = width // nx
    groups = length // LANES
    down_steps, up_steps = nz // 2, nz // 2 - 1
    per_part = nx // parts
    row, col = lax.axis_index("row"), lax.axis_index("col")
    x, z = row // nz, lax.rem(row, nz)
    y, core = col // nc, lax.rem(col, nc)

    def at(px, pz, pc):
        return {"row": px * nz + pz, "col": pc}

    def x_peer(k):
        return lax.rem(x + k, nx)

    def z_peer(k):
        return lax.rem(z + k, nz)

    def copy(src, dst, send, recv, where):
        return pltpu.make_async_remote_copy(
            src_ref=src, dst_ref=dst, send_sem=send, recv_sem=recv,
            device_id=where, device_id_type=MESH,
        )

    load = pltpu.make_async_copy(panel_ref, panel, panel_sem)
    load.start()

    barrier = pltpu.get_barrier_semaphore()

    def greet(where):
        pl.semaphore_signal(barrier, inc=1, device_id=where, device_id_type=MESH)

    for k in range(1, nx):
        greet(at(x_peer(k), z, col))
    for k in range(1, nz):
        greet(at(x, z_peer(k), col))
    for k in range(1, ny * nc):
        greet(at(x, z, lax.rem(col + k, ny * nc)))
    for k in range(nx):
        for dc in range(nc):
            where = at(x_peer(k), z, x * nc + lax.rem(core + dc, nc))
            if k == 0 and dc == 0:
                @pl.when(x != y)
                def _():
                    greet(where)
            else:
                greet(where)

    samples[z, x] = samp_ref[...]
    load.wait()
    for jh in range(groups):
        lanes = slice(jh * LANES, (jh + 1) * LANES)
        sign = signs_ref[jh : jh + 1, :].astype(jnp.float32)
        signed = panel[:, lanes] * sign
        for d in range(nx):
            xs[d, jh * block : (jh + 1) * block, :] = signed[d * block : (d + 1) * block]
    greeted = nx - 1 + nz - 1 + ny * nc - 1 + nx * nc
    pl.semaphore_wait(barrier, greeted - jnp.where(x == y, 1, 0))

    sx = [copy(samples.at[z, x], samples.at[z, x], sx_send.at[k], sx_recv.at[k], at(x_peer(k), z, col)) for k in range(1, nx)]
    for c in sx:
        c.start()
    xc = [copy(xs.at[x_peer(k)], xr.at[x], x_send.at[k], x_recv.at[k], at(x_peer(k), z, col)) for k in range(1, nx)]
    for c in xc:
        c.start()
    xr[x] = xs[x]
    for k in range(1, nx):
        copy(samples.at[z, x], samples.at[z, x_peer(nx - k)], sx_send.at[k], sx_recv.at[k], at(x_peer(k), z, col)).wait_recv()

    def sz(k):
        return copy(samples.at[z], samples.at[z], sz_send.at[k], sz_recv.at[k], at(x, z_peer(k), col))

    @pl.loop(1, nz)
    def _(k):
        sz(k).start()

    lane_bits = lax.broadcasted_iota(jnp.int32, (8, LANES), 0)
    high_bits = lax.broadcasted_iota(jnp.int32, (groups, LANES), 0)

    def tables(t):
        both = z * 0
        for b in range(nz.bit_length() - 1):
            both = both + lax.rem(z // (1 << b), 2) * lax.rem(t // (1 << b), 2)
        z_sign = (1 - 2 * lax.rem(both, 2)).astype(jnp.float32)
        for xx in range(nx):
            place = samples[t, xx]
            base = parity_sign(lane_bits & place)
            wide = [base]
            for b in range(3, 7):
                factor = (1 - 2 * ((place >> b) & 1)).astype(jnp.float32)
                wide = wide + [w * factor for w in wide]
            had[t, xx] = jnp.concatenate(wide, axis=0).astype(jnp.bfloat16)
            mask[t, xx] = parity_sign(high_bits & (place >> 7)) * z_sign

    tables(z)

    @pl.loop(1, nz)
    def _(k):
        src = z_peer(nz - k)
        copy(samples.at[src], samples.at[src], sz_send.at[k], sz_recv.at[k], at(x, z_peer(k), col)).wait_recv()
        tables(src)

    for k in range(1, nx):
        copy(xs.at[x_peer(k)], xr.at[x_peer(nx - k)], x_send.at[k], x_recv.at[k], at(x_peer(k), z, col)).wait_recv()
    for jh in range(groups):
        part = slice(jh * block, (jh + 1) * block)
        for xx, value in enumerate(butterfly([xr[d, part] for d in range(nx)])):
            hi, lo = split_hi_lo(value)
            mixed[xx, part, :LANES] = hi
            mixed[xx, part, LANES:] = lo

    def dn(k, p):
        span = pl.ds(p * per_part, per_part)
        return copy(send_dn.at[k, span], recv_dn.at[k, span], dn_send.at[k, p], dn_recv.at[k, p], at(x, z_peer(nz - 1), col))

    def up(k, p):
        span = pl.ds(p * per_part, per_part)
        return copy(send_up.at[k, span], recv_up.at[k, span], up_send.at[k, p], up_recv.at[k, p], at(x, z_peer(1), col))

    @pl.loop(0, down_steps)
    def _(k):
        t_dn = lax.rem(z + nz - down_steps + k, nz)
        t_up = lax.rem(z + up_steps - k, nz)
        for xx in range(nx):
            table = jnp.concatenate([had[t_dn, xx], had[t_up, xx]], axis=1)
            table = jnp.concatenate([table, table], axis=0)
            product = jnp.dot(mixed[xx], table, preferred_element_type=jnp.float32)
            signs_dn, signs_up = mask[t_dn, xx], mask[t_up, xx]
            total_dn = total_up = None
            for jh in range(groups):
                part = product[jh * block : (jh + 1) * block]
                term_dn = part[:, :LANES] * signs_dn[jh : jh + 1]
                term_up = part[:, LANES:] * signs_up[jh : jh + 1]
                total_dn = term_dn if jh == 0 else total_dn + term_dn
                total_up = term_up if jh == 0 else total_up + term_up
            send_dn[k, xx] = total_dn
            send_up[k, xx] = total_up
        for p in range(parts):
            span = pl.ds(p * per_part, per_part)

            @pl.when(k > 0)
            def _():
                dn(k - 1, p).wait_recv()
                send_dn[k, span] = send_dn[k, span] + recv_dn[k - 1, span]

            dn(k, p).start()

            @pl.when(k > 0)
            def _():
                up(k - 1, p).wait_recv()
                send_up[k, span] = send_up[k, span] + recv_up[k - 1, span]

            @pl.when(k < up_steps)
            def _():
                up(k, p).start()

    scale = 1.0 / jnp.sqrt(jnp.float32(length * nx * nz))
    for p in range(parts):
        span = pl.ds(p * per_part, per_part)
        dn(down_steps - 1, p).wait_recv()
        own[x, span] = (send_up[up_steps, span] + recv_dn[down_steps - 1, span]) * scale

    def own_copy(k):
        return copy(own.at[x], own.at[x], own_send.at[k], own_recv.at[k], at(x_peer(k), z, col))

    def row_copy(dy, dc):
        where = at(y, z, lax.rem(y + dy, ny) * nc + lax.rem(core + dc, nc))
        return copy(own.at[x], rows.at[core, x], row_send.at[dy, dc], row_recv.at[dc, x], where)

    for k in range(1, nx):
        own_copy(k).start()
    for dy in range(ny):
        for dc in range(nc):
            if dy == 0 and dc == 0:
                @pl.when(x != y)
                def _():
                    row_copy(0, 0).start()

                @pl.when(x == y)
                def _():
                    rows[core, x] = own[x]
            else:
                row_copy(dy, dc).start()
    for k in range(1, nx):
        src = x_peer(nx - k)
        copy(own.at[x], own.at[src], own_send.at[k], own_recv.at[k], at(x_peer(k), z, col)).wait_recv()
    for b in range(nx):
        sketch_ref[b * block : (b + 1) * block, :] = own[b, x]
    for k in range(nx):
        for dc in range(nc):
            src = x_peer(k)
            incoming = copy(
                own.at[x], rows.at[lax.rem(core + nc - dc, nc), src], row_send.at[0, dc], row_recv.at[dc, src],
                at(y, z, lax.rem(y + 1, ny) * nc + core),
            )
            if k == 0 and dc == 0:
                @pl.when(x != y)
                def _():
                    incoming.wait_recv()
            else:
                incoming.wait_recv()

    total = None
    blank = jnp.zeros((width, LANES), jnp.float32)
    for b in range(nx):
        left = jnp.concatenate([rows[c, d, b] for c in range(nc) for d in range(nx)], axis=0)
        right = jnp.concatenate([own[d, b] for d in range(nx)], axis=0)
        first = jnp.where(core == 0, right, blank)
        right = jnp.concatenate([first, right - first], axis=0)
        left_hi, left_lo = split_hi_lo(left)
        right_hi, right_lo = split_hi_lo(right)
        term = lax.dot_general(
            jnp.concatenate([left_hi, left_hi, left_lo], axis=1),
            jnp.concatenate([right_hi, right_lo, right_hi], axis=1),
            (((1,), (1,)), ((), ())),
            preferred_element_type=jnp.float32,
        )
        total = term if b == 0 else total + term
    tile[...] = total.reshape(tile.shape)

    def gz(k):
        return copy(tile.at[z_peer(k)], tile_in.at[k], gz_send.at[k], gz_recv.at[k], at(x, z_peer(k), col))

    @pl.loop(1, nz)
    def _(k):
        gz(k).start()

    total = tile[z]
    for k in range(1, nz):
        gz(k).wait_recv()
        total = total + tile_in[k]
    final[col] = total * (1.0 / (LANES * nx * nz))

    def gc(k):
        return copy(final.at[col], final.at[col], gc_send.at[k], gc_recv.at[k], at(x, z, lax.rem(col + k, ny * nc)))

    for k in range(1, ny * nc):
        gc(k).start()
    for k in range(1, ny * nc):
        src = lax.rem(col + ny * nc - k, ny * nc)
        copy(final.at[col], final.at[src], gc_send.at[k], gc_recv.at[k], at(x, z, lax.rem(col + k, ny * nc))).wait_recv()
    for b in range(ny):
        both = final[b * nc]
        for c in range(1, nc):
            both = both + final[b * nc + c]
        gram_ref[:, b * LANES : (b + 1) * LANES] = both

    for c in sx + xc:
        c.wait_send()

    @pl.loop(1, nz)
    def _(k):
        sz(k).wait_send()
        gz(k).wait_send()

    @pl.loop(0, down_steps)
    def _(k):
        for p in range(parts):
            dn(k, p).wait_send()

            @pl.when(k < up_steps)
            def _():
                up(k, p).wait_send()

    for k in range(1, nx):
        own_copy(k).wait_send()
    for dy in range(ny):
        for dc in range(nc):
            if dy == 0 and dc == 0:
                @pl.when(x != y)
                def _():
                    row_copy(0, 0).wait_send()
            else:
                row_copy(dy, dc).wait_send()
    for k in range(1, ny * nc):
        gc(k).wait_send()


def per_device(dims, panel, signs, sample_rows):
    nx, nz, ny, nc, parts = dims
    width, length = panel.shape
    block, groups = width // nx, length // LANES
    gram_rows = width * nc // nz
    place = jnp.bitwise_and(sample_rows, length - 1).reshape(1, LANES)
    f32, bf16 = jnp.float32, jnp.bfloat16
    vmem, dma = pltpu.VMEM, pltpu.SemaphoreType.DMA
    down, up = nz // 2, nz // 2 - 1
    return pl.pallas_call(
        functools.partial(kernel, dims),
        out_shape=(
            jax.ShapeDtypeStruct((width, LANES), f32),
            jax.ShapeDtypeStruct((gram_rows, width * ny * nc), f32),
        ),
        in_specs=[
            pl.BlockSpec(memory_space=pl.ANY),
            pl.BlockSpec(memory_space=vmem),
            pl.BlockSpec(memory_space=vmem),
        ],
        out_specs=(pl.BlockSpec(memory_space=vmem), pl.BlockSpec(memory_space=vmem)),
        scratch_shapes=[
            vmem((width, length), f32),
            vmem((nx, groups * block, LANES), f32),
            vmem((nx, groups * block, LANES), f32),
            vmem((nz, nx, 1, LANES), jnp.int32),
            vmem((nz, nx, LANES, LANES), bf16),
            vmem((nz, nx, groups, LANES), f32),
            vmem((nx, groups * block, 2 * LANES), bf16),
            vmem((down, nx, block, LANES), f32),
            vmem((down, nx, block, LANES), f32),
            vmem((down, nx, block, LANES), f32),
            vmem((down, nx, block, LANES), f32),
            vmem((nx, nx, block, LANES), f32),
            vmem((nc, nx, nx, block, LANES), f32),
            vmem((nz, gram_rows, LANES), f32),
            vmem((nz, gram_rows, LANES), f32),
            vmem((ny * nc, gram_rows, LANES), f32),
            dma, dma((nx,)), dma((nx,)), dma((nz,)), dma((nz,)), dma((nx,)), dma((nx,)),
            dma((down, parts)), dma((down, parts)), dma((down, parts)), dma((down, parts)),
            dma((nx,)), dma((nx,)), dma((ny, nc)), dma((nc, nx)),
            dma((nz,)), dma((nz,)), dma((ny * nc,)), dma((ny * nc,)),
        ],
        compiler_params=pltpu.CompilerParams(
            collective_id=0, has_side_effects=True, vmem_limit_bytes=32 * 1024 * 1024
        ),
        cost_estimate=pl.CostEstimate(flops=1 << 30, bytes_accessed=1 << 20, transcendentals=0),
    )(panel, signs.reshape(groups, LANES), place)


def build(mesh, dims):
    return jax.shard_map(
        functools.partial(per_device, dims),
        mesh=mesh,
        in_specs=(P("col", "row"), P("row"), P("row")),
        out_specs=(P("col", "row"), P("row", None)),
        check_vma=False,
    )


def solution(mesh):
    return build(mesh, (4, 16, 4, 2, 2))
```

time: 497 us -> 79.7 us (0.16)
  waiting for transfers between devices: 375 us -> 0 us
  Pallas kernels: 0 us -> 75.2 us
  starting transfers between devices: 54.7 us -> 0 us
  blocking collectives: 38.9 us -> 0 us
  between operations: 15 us -> 0.65 us
  local copies, waits for them, and re-layouts: 8.7 us -> 3.61 us
    unnamed x2 -> x0, waiting for transfers between devices: 262 us -> none
    ppermute x6 -> x0, waiting for transfers between devices: 113 us -> none  [partner(): return lax.ppermute(value, axis, pairs)]
    pallas_call x0 -> x1, Pallas kernels: none -> 75.2 us  [per_device(): pl.pallas_call(functools.partial(kernel, dims), out_shape=(jax.ShapeDtype...]
    ppermute x6 -> x0, starting transfers between devices: 54.6 us -> none  [partner(): return lax.ppermute(value, axis, pairs)]
    all_gather x2 -> x0, blocking collectives: 38.9 us -> none  [the longest x1 23.5 us: per_device(): gram = lax.all_gather(my_block, 'col', axis=1, tiled=True)]
  transfers between devices with their start and end apart: 7 -> 0, of which waited for: 7 -> 0; matrix products, arithmetic and copies ran while one was open for 0% -> 0% of each run, Pallas kernels for 0% -> 0%
where the time goes in v1:
time: 79.7 us; the launch traced here: 79.5 us
  Pallas kernels  75.2 us (94%)
  local copies, waits for them, and re-layouts  3.61 us (5%)
    pallas_call x1, Pallas kernels, per_device(): pl.pallas_call(functools.partial(kernel, dims), out_shape=(jax.ShapeDtype...  75.2 us
    unnamed x8, local copies, waits for them, and re-layouts  3.61 us

profile of v1, /device:TPU:1, one launch (start us, length us, event | category | flops | bytes accessed | tf_op | source)
XLA Modules:
  0.0 79.5 jit_solution(6268028584977496740)
XLA Ops:
  0.6 0.0 copy-start.2
  0.6 0.6 copy-done.2
  1.3 0.0 copy-start
  1.3 1.0 %copy-done = f32[64,2048]{1,0:T(8,128)S(1)} copy-done((f32[64,2048]{1,0:T(8,128)S(1)}, f32[64,2048]{1,0:T(8,128)}, u32[]{:S(2)}) %copy-start) | copy-done | bytes 524312
  2.3 0.0 copy-start.1
  2.3 0.7 copy-done.1
  3.0 75.2 %shard_map.50 = (f32[64,128]{1,0:T(8,128)S(1)}, f32[8,512]{1,0:T(8,128)S(1)}) custom-call(f32[64,2048]{1,0:T(8,128)S(1)} %copy-done, s32[16,128]{1,0:T(8,128)S(1)} %bitcast.3, s32[1,128]{1,0:T(1,128)S(1)} %and_bitcast_fusion.samp_ref), custom_call_target="tpu_custom_call" | custom-call | flops 1073741824 | bytes 1048576 | tf_op jit(solution)/shard_map/pallas_call | solution.py:334
  78.2 0.6 copy.7
  78.9 0.6 copy.8
  (1 shorter events, 0.0 us)
Async XLA Ops:
  0.6 0.7 copy-start.2
  1.3 1.0 %copy-start = (f32[64,2048]{1,0:T(8,128)S(1)}, f32[64,2048]{1,0:T(8,128)}, u32[]{:S(2)}) copy-start(f32[64,2048]{1,0:T(8,128)} %panel_ref.1) | copy-start | bytes 1572868
  2.3 0.7 copy-start.1

commit v2 on v0

v2 whole, which is shorter than its diff:
```python
import functools

import jax
import jax.numpy as jnp
from jax import lax
from jax.experimental import pallas as pl
from jax.experimental.pallas import tpu as pltpu
from jax.sharding import PartitionSpec as P

MESH = pl.DeviceIdType.MESH
LANES = 128


def parity_sign(bits):
    bits = bits ^ (bits >> 4)
    bits = bits ^ (bits >> 2)
    bits = bits ^ (bits >> 1)
    return (1 - 2 * (bits & 1)).astype(jnp.float32)


def split_hi_lo(value):
    hi = value.astype(jnp.bfloat16)
    return hi, (value - hi.astype(jnp.float32)).astype(jnp.bfloat16)


def butterfly(blocks):
    blocks = list(blocks)
    step = 1
    while step < len(blocks):
        for first in range(len(blocks)):
            if not first & step:
                low, high = blocks[first], blocks[first + step]
                blocks[first], blocks[first + step] = low + high, low - high
        step *= 2
    return blocks


def kernel(
    dims, panel_ref, signs_ref, samp_ref, sketch_ref, gram_ref,
    panel, signs, samp, xs, xr, samples, had, mask, mixed, part_out, part_in,
    own, rows, tile, tile_in, final, gathered,
    load_sem, s1_send, s1_recv, s2_send, s2_recv, x_send, x_recv, p_send, p_recv,
    own_send, own_recv, row_send, row_recv, t_send, t_recv, f_send, f_recv,
):
    nx, nz, ny, nc = dims
    width, length = panel.shape
    near, far, cols = 2 * nx, nz // 2, ny * nc
    turns = nz // near
    block = width // near
    groups = length // LANES
    row, col = lax.axis_index("row"), lax.axis_index("col")
    x, z = row // nz, lax.rem(row, nz)
    zh, zl = z // 2, lax.rem(z, 2)
    g = 2 * x + zl

    def copy(src, dst, send, recv, where):
        return pltpu.make_async_remote_copy(
            src_ref=src, dst_ref=dst, send_sem=send, recv_sem=recv,
            device_id=where, device_id_type=MESH,
        )

    def near_id(k):
        return lax.rem(g + k, near)

    def near_at(k):
        other = near_id(k)
        return {"row": (other // 2) * nz + 2 * zh + lax.rem(other, 2), "col": col}

    def far_id(k):
        return lax.rem(zh + k, far)

    def far_at(k):
        return {"row": x * nz + 2 * far_id(k) + zl, "col": col}

    def col_id(k):
        return lax.rem(col + k, cols)

    def col_at(k):
        return {"row": row, "col": col_id(k)}

    hub = lax.rem(zh, nx)

    loads = [
        pltpu.make_async_copy(src, dst, load_sem.at[i])
        for i, (src, dst) in enumerate([(samp_ref, samp), (signs_ref, signs), (panel_ref, panel)])
    ]
    for c in loads:
        c.start()

    barrier = pltpu.get_barrier_semaphore()

    def greet(where):
        pl.semaphore_signal(barrier, inc=1, device_id=where, device_id_type=MESH)

    for k in range(1, near):
        greet(near_at(k))
    for k in range(1, far):
        greet(far_at(k))
    for k in range(1, cols):
        greet(col_at(k))

    @pl.when(x != hub)
    def _():
        for k in range(cols):
            greet({"row": hub * nz + z, "col": col_id(k)})

    for c in loads:
        c.wait()
    samples[zh, g] = samp[...] & (length - 1)
    for jh in range(groups):
        sign = signs[jh : jh + 1, :].astype(jnp.float32)
        signed = panel[:, jh * LANES : (jh + 1) * LANES] * sign
        for d in range(near):
            xs[d, jh * block : (jh + 1) * block, :] = signed[d * block : (d + 1) * block]
    greeted = near - 1 + far - 1 + cols - 1
    pl.semaphore_wait(barrier, greeted + jnp.where(x == hub, (nx - 1) * cols, 0))
    def s1(k):
        return copy(samples.at[zh, g], samples.at[zh, g], s1_send.at[k], s1_recv.at[k], near_at(k))

    def s2(k):
        return copy(samples.at[zh], samples.at[zh], s2_send.at[k], s2_recv.at[k], far_at(k))

    def xc(k):
        return copy(xs.at[near_id(k)], xr.at[g], x_send.at[k], x_recv.at[k], near_at(k))

    for k in range(1, near):
        s1(k).start()
    for k in range(1, near):
        xc(k).start()
    xr[g] = xs[g]
    for k in range(1, near):
        src = near_id(near - k)
        copy(samples.at[zh, g], samples.at[zh, src], s1_send.at[k], s1_recv.at[k], near_at(k)).wait_recv()
    for k in range(1, far):
        s2(k).start()

    lane_bits = lax.broadcasted_iota(jnp.int32, (8, LANES), 0)
    high_bits = lax.broadcasted_iota(jnp.int32, (groups, LANES), 0)

    def tables(t):
        both = zh * 0
        for b in range(far.bit_length() - 1):
            both = both + lax.rem(zh // (1 << b), 2) * lax.rem(t // (1 << b), 2)
        far_sign = (1 - 2 * lax.rem(both, 2)).astype(jnp.float32)

        @pl.loop(0, near)
        def _(i):
            place = samples[t, i]
            wide = [parity_sign(lane_bits & place)]
            for b in range(3, 7):
                factor = (1 - 2 * ((place >> b) & 1)).astype(jnp.float32)
                wide = wide + [w * factor for w in wide]
            had[t, i] = jnp.concatenate(wide, axis=0).astype(jnp.bfloat16)
            mask[t, i] = parity_sign(high_bits & (place >> 7)) * far_sign

    tables(zh)
    for k in range(1, far):
        src = far_id(far - k)
        copy(samples.at[zh], samples.at[src], s2_send.at[k], s2_recv.at[k], far_at(k)).wait_recv()
        tables(src)

    for k in range(1, near):
        src = near_id(near - k)
        copy(xs.at[g], xr.at[src], x_send.at[k], x_recv.at[k], near_at(k)).wait_recv()
    for jh in range(groups):
        part = slice(jh * block, (jh + 1) * block)
        for i, value in enumerate(butterfly([xr[d, part] for d in range(near)])):
            hi, lo = split_hi_lo(value)
            mixed[i, part, :LANES] = hi
            mixed[i, part, LANES:] = lo
    def pc(k):
        return copy(part_out.at[k], part_in.at[k], p_send.at[k], p_recv.at[k], far_at(k))

    order = sorted(range(far), key=lambda k: -min(k, far - k))
    for first, second in zip(order[::2], order[1::2]):
        targets = (far_id(first), far_id(second))

        @pl.loop(0, near)
        def _(i):
            table = jnp.concatenate([had[t, i] for t in targets], axis=1)
            table = jnp.concatenate([table, table], axis=0)
            product = jnp.dot(mixed[i], table, preferred_element_type=jnp.float32)
            for n, (k, t) in enumerate(zip((first, second), targets)):
                signs_t = mask[t, i]
                total = None
                for jh in range(groups):
                    term = product[jh * block : (jh + 1) * block, n * LANES : (n + 1) * LANES] * signs_t[jh : jh + 1]
                    total = term if jh == 0 else total + term
                part_out[k, i] = total

        for k in (first, second):
            if k:
                pc(k).start()
    total = part_out[0]
    for k in reversed([k for k in order if k]):
        pc(k).wait_recv()
        total = total + part_in[k]
    own[g] = total * (1.0 / jnp.sqrt(jnp.float32(length * nx * nz)))
    def own_copy(k):
        return copy(own.at[g], own.at[g], own_send.at[k], own_recv.at[k], near_at(k))

    def row_copy(k):
        return copy(own.at[g], rows.at[col], row_send.at[k], row_recv.at[k], col_at(k))

    for k in range(1, cols):
        row_copy(k).start()
    for k in range(1, near):
        own_copy(k).start()
    rows[col] = own[g]
    for k in range(1, cols):
        src = col_id(cols - k)
        copy(own.at[g], rows.at[src], row_send.at[k], row_recv.at[k], col_at(k)).wait_recv()
    for k in range(1, near):
        src = near_id(near - k)
        copy(own.at[g], own.at[src], own_send.at[k], own_recv.at[k], near_at(k)).wait_recv()
    total = None
    blank = jnp.zeros((width, LANES), jnp.float32)
    odd = lax.rem(col, 2)
    for b in range(near):
        left = jnp.concatenate([rows[turns * d + m, b] for m in range(turns) for d in range(nx)], axis=0)
        right = jnp.concatenate([own[d, b] for d in range(near)], axis=0)
        first = jnp.where(odd == 0, right, blank)
        right = jnp.concatenate([first, right - first], axis=0)
        left_hi, left_lo = split_hi_lo(left)
        right_hi, right_lo = split_hi_lo(right)
        term = lax.dot_general(
            jnp.concatenate([left_hi, left_hi, left_lo], axis=1),
            jnp.concatenate([right_hi, right_lo, right_hi], axis=1),
            (((1,), (1,)), ((), ())),
            preferred_element_type=jnp.float32,
        )
        total = term if b == 0 else total + term
    tile[...] = total.reshape(tile.shape)

    def tc(m):
        target = nx * m + x
        return copy(
            tile.at[m], tile_in.at[zh], t_send.at[m], t_recv.at[zh], {"row": x * nz + 2 * target + zl, "col": col}
        )

    for m in range(turns):
        @pl.when(zh != nx * m + x)
        def _():
            tc(m).start()
    for d in range(near):
        sketch_ref[d * block : (d + 1) * block, :] = own[d, g]

    def fc(kx, kc):
        dest = lax.rem(x + kx, nx)
        return copy(
            final.at[dest], gathered.at[col], f_send.at[kx, kc], f_recv.at[col], {"row": dest * nz + z, "col": col_id(kc)}
        )

    @pl.when(x == hub)
    def _():
        total = tile[zh // nx]
        for k in range(1, far):
            src = far_id(far - k)
            copy(tile.at[0], tile_in.at[src], t_send.at[0], t_recv.at[src], far_at(k)).wait_recv()
            total = total + tile_in[src]
        final[...] = total * (1.0 / (LANES * nx * nz))
        gathered[col] = final[x]
        for kx in range(nx - 1, -1, -1):
            for kc in range(cols):
                if kx or kc:
                    fc(kx, kc).start()
    def incoming(k):
        src = col_id(k)
        return copy(final.at[0], gathered.at[src], f_send.at[0, k], f_recv.at[src], col_at(k))

    for k in range(1, cols):
        incoming(k).wait_recv()

    @pl.when(x != hub)
    def _():
        copy(final.at[0], gathered.at[col], f_send.at[0, 1], f_recv.at[col], col_at(1)).wait_recv()

    for b in range(cols // 2):
        gram_ref[:, b * LANES : (b + 1) * LANES] = gathered[2 * b] + gathered[2 * b + 1]

    for k in range(1, near):
        s1(k).wait_send()
        xc(k).wait_send()
        own_copy(k).wait_send()
    for k in range(1, far):
        s2(k).wait_send()
        pc(k).wait_send()
    for k in range(1, cols):
        row_copy(k).wait_send()
    for m in range(turns):
        @pl.when(zh != nx * m + x)
        def _():
            tc(m).wait_send()

    @pl.when(x == hub)
    def _():
        for kx in range(nx):
            for kc in range(cols):
                if kx or kc:
                    fc(kx, kc).wait_send()


def per_device(dims, panel, signs, sample_rows):
    nx, nz, ny, nc = dims
    near, far, cols = 2 * nx, nz // 2, ny * nc
    turns = nz // near
    width, length = panel.shape
    block, groups = width // near, length // LANES
    f32, bf16, i32 = jnp.float32, jnp.bfloat16, jnp.int32
    vmem, dma = pltpu.VMEM, pltpu.SemaphoreType.DMA
    return pl.pallas_call(
        functools.partial(kernel, dims),
        out_shape=(
            jax.ShapeDtypeStruct((width, LANES), f32),
            jax.ShapeDtypeStruct((block, width * cols), f32),
        ),
        in_specs=[pl.BlockSpec(memory_space=pl.ANY)] * 3,
        out_specs=(pl.BlockSpec(memory_space=vmem), pl.BlockSpec(memory_space=vmem)),
        scratch_shapes=[
            vmem((width, length), f32),
            vmem((groups, LANES), i32),
            vmem((1, LANES), i32),
            vmem((near, groups * block, LANES), f32),
            vmem((near, groups * block, LANES), f32),
            vmem((far, near, 1, LANES), i32),
            vmem((far, near, LANES, LANES), bf16),
            vmem((far, near, groups, LANES), f32),
            vmem((near, groups * block, 2 * LANES), bf16),
            vmem((far, near, block, LANES), f32),
            vmem((far, near, block, LANES), f32),
            vmem((near, near, block, LANES), f32),
            vmem((cols, near, block, LANES), f32),
            vmem((turns, nx, block, LANES), f32),
            vmem((far, nx, block, LANES), f32),
            vmem((nx, block, LANES), f32),
            vmem((cols, block, LANES), f32),
            dma((3,)), dma((near,)), dma((near,)), dma((far,)), dma((far,)), dma((near,)), dma((near,)),
            dma((far,)), dma((far,)), dma((near,)), dma((near,)), dma((cols,)), dma((cols,)),
            dma((turns,)), dma((far,)), dma((nx, cols)), dma((cols,)),
        ],
        compiler_params=pltpu.CompilerParams(
            collective_id=0, has_side_effects=True, vmem_limit_bytes=60 * 1024 * 1024
        ),
        cost_estimate=pl.CostEstimate(flops=1 << 30, bytes_accessed=1 << 20, transcendentals=0),
    )(panel, signs.reshape(groups, LANES), sample_rows.reshape(1, LANES))


def build(mesh, dims):
    return jax.shard_map(
        functools.partial(per_device, dims),
        mesh=mesh,
        in_specs=(P("col", "row"), P("row"), P("row")),
        out_specs=(P("col", "row"), P("row", None)),
        check_vma=False,
    )


def solution(mesh):
    return build(mesh, (4, 16, 4, 2))
```

time: 497 us -> 66.5 us (0.13)
  waiting for transfers between devices: 375 us -> 0 us
  Pallas kernels: 0 us -> 63.7 us
  starting transfers between devices: 54.7 us -> 0 us
  blocking collectives: 38.9 us -> 0 us
  between operations: 15 us -> 0.65 us
  local copies, waits for them, and re-layouts: 8.7 us -> 1.99 us
    unnamed x2 -> x0, waiting for transfers between devices: 262 us -> none
    ppermute x6 -> x0, waiting for transfers between devices: 113 us -> none  [partner(): return lax.ppermute(value, axis, pairs)]
    pallas_call x0 -> x1, Pallas kernels: none -> 63.7 us  [per_device(): pl.pallas_call(functools.partial(kernel, dims), out_shape=(jax.ShapeDtype...]
    ppermute x6 -> x0, starting transfers between devices: 54.6 us -> none  [partner(): return lax.ppermute(value, axis, pairs)]
    all_gather x2 -> x0, blocking collectives: 38.9 us -> none  [the longest x1 23.5 us: per_device(): gram = lax.all_gather(my_block, 'col', axis=1, tiled=True)]
  transfers between devices with their start and end apart: 7 -> 0, of which waited for: 7 -> 0; matrix products, arithmetic and copies ran while one was open for 0% -> 0% of each run, Pallas kernels for 0% -> 0%
where the time goes in v2:
time: 66.5 us; the launch traced here: 66.3 us
  Pallas kernels  63.7 us (96%)
  local copies, waits for them, and re-layouts  1.99 us (3%)
    pallas_call x1, Pallas kernels, per_device(): pl.pallas_call(functools.partial(kernel, dims), out_shape=(jax.ShapeDtype...  63.7 us
    unnamed x4, local copies, waits for them, and re-layouts  1.99 us

profile of v2, /device:TPU:1, one launch (start us, length us, event | category | flops | bytes accessed | tf_op | source)
XLA Modules:
  0.0 66.3 jit_solution(3266331324144267240)
XLA Ops:
  0.6 63.7 %shard_map.50 = (f32[64,128]{1,0:T(8,128)}, f32[8,512]{1,0:T(8,128)}) custom-call(f32[64,2048]{1,0:T(8,128)} %panel_ref.1, s32[16,128]{1,0:T(8,128)} %bitcast.2, s32[1,128]{1,0:T(1,128)} %bitcast.3), custom_call_target="tpu_custom_call" | custom-call | flops 1073741824 | bytes 1048576 | tf_op jit(solution)/shard_map/pallas_call | solution.py:311
  64.3 0.0 copy-start
  64.3 1.4 %copy.7 = f32[64,128]{1,0:T(8,128)} copy(f32[64,128]{1,0:T(8,128)} %get-tuple-element.4) | data formatting | bytes 65536
  65.7 0.0 copy-done
  65.7 0.6 copy.8
Async XLA Ops:
  64.3 1.4 %copy-start = (f32[8,512]{1,0:T(8,128)S(1)}, f32[8,512]{1,0:T(8,128)}, u32[]{:S(2)}) copy-start(f32[8,512]{1,0:T(8,128)} %get-tuple-element.5) | copy-start | bytes 49156

commit v3 on v2

--- a/solution.py
+++ b/solution.py
@@ -39,7 +39,7 @@
     dims, panel_ref, signs_ref, samp_ref, sketch_ref, gram_ref,
     panel, signs, samp, xs, xr, samples, had, mask, mixed, part_out, part_in,
     own, rows, tile, tile_in, final, gathered,
-    load_sem, s1_send, s1_recv, s2_send, s2_recv, x_send, x_recv, p_send, p_recv,
+    load_sem, s_send, s_recv, pass_send, pass_recv, x_send, x_recv, p_send, p_recv,
     own_send, own_recv, row_send, row_recv, t_send, t_recv, f_send, f_recv,
 ):
     nx, nz, ny, nc = dims
@@ -80,6 +80,10 @@
 
     hub = lax.rem(zh, nx)
 
+    slots = sorted(range(far), key=lambda k: (min(k, far - k), k))
+    close = 1 + sum(0 < min(k, far - k) <= far // 4 for k in slots)
+    batches = [(0, 1), (1, close), (close, far)]
+
     loads = [
         pltpu.make_async_copy(src, dst, load_sem.at[i])
         for i, (src, dst) in enumerate([(samp_ref, samp), (signs_ref, signs), (panel_ref, panel)])
@@ -92,72 +96,77 @@
     def greet(where):
         pl.semaphore_signal(barrier, inc=1, device_id=where, device_id_type=MESH)
 
+    for k in reversed(slots[1:]):
+        greet(far_at(k))
     for k in range(1, near):
         greet(near_at(k))
-    for k in range(1, far):
-        greet(far_at(k))
     for k in range(1, cols):
         greet(col_at(k))
 
-    @pl.when(x != hub)
-    def _():
-        for k in range(cols):
-            greet({"row": hub * nz + z, "col": col_id(k)})
-
     for c in loads:
         c.wait()
-    samples[zh, g] = samp[...] & (length - 1)
+    samples[g, 0] = samp[...]
     for jh in range(groups):
         sign = signs[jh : jh + 1, :].astype(jnp.float32)
         signed = panel[:, jh * LANES : (jh + 1) * LANES] * sign
         for d in range(near):
             xs[d, jh * block : (jh + 1) * block, :] = signed[d * block : (d + 1) * block]
-    greeted = near - 1 + far - 1 + cols - 1
-    pl.semaphore_wait(barrier, greeted + jnp.where(x == hub, (nx - 1) * cols, 0))
-    def s1(k):
-        return copy(samples.at[zh, g], samples.at[zh, g], s1_send.at[k], s1_recv.at[k], near_at(k))
-
-    def s2(k):
-        return copy(samples.at[zh], samples.at[zh], s2_send.at[k], s2_recv.at[k], far_at(k))
+    pl.semaphore_wait(barrier, near - 1 + far - 1 + cols - 1)
+    def sc(k):
+        return copy(samp, samples.at[g, slots.index((far - k) % far)], s_send.at[k], s_recv.at[k], far_at(k))
+
+    def sc_wait(k):
+        copy(samp, samples.at[g, slots.index(k)], s_send.at[k], s_recv.at[far - k], far_at(k)).wait_recv()
+
+    def hand_on(b, k, whose):
+        first, end = batches[b]
+        span = samples.at[whose, pl.ds(first, end - first)]
+        return copy(span, span, pass_send.at[b, k], pass_recv.at[b, k], near_at(k))
 
     def xc(k):
         return copy(xs.at[near_id(k)], xr.at[g], x_send.at[k], x_recv.at[k], near_at(k))
 
-    for k in range(1, near):
-        s1(k).start()
+    for k in reversed(slots[1:]):
+        sc(k).start()
+    for k in range(1, near):
+        hand_on(0, k, g).start()
     for k in range(1, near):
         xc(k).start()
     xr[g] = xs[g]
-    for k in range(1, near):
-        src = near_id(near - k)
-        copy(samples.at[zh, g], samples.at[zh, src], s1_send.at[k], s1_recv.at[k], near_at(k)).wait_recv()
-    for k in range(1, far):
-        s2(k).start()
 
     lane_bits = lax.broadcasted_iota(jnp.int32, (8, LANES), 0)
     high_bits = lax.broadcasted_iota(jnp.int32, (groups, LANES), 0)
 
-    def tables(t):
-        both = zh * 0
-        for b in range(far.bit_length() - 1):
-            both = both + lax.rem(zh // (1 << b), 2) * lax.rem(t // (1 << b), 2)
-        far_sign = (1 - 2 * lax.rem(both, 2)).astype(jnp.float32)
-
-        @pl.loop(0, near)
-        def _(i):
-            place = samples[t, i]
-            wide = [parity_sign(lane_bits & place)]
-            for b in range(3, 7):
-                factor = (1 - 2 * ((place >> b) & 1)).astype(jnp.float32)
-                wide = wide + [w * factor for w in wide]
-            had[t, i] = jnp.concatenate(wide, axis=0).astype(jnp.bfloat16)
-            mask[t, i] = parity_sign(high_bits & (place >> 7)) * far_sign
-
-    tables(zh)
-    for k in range(1, far):
-        src = far_id(far - k)
-        copy(samples.at[zh], samples.at[src], s2_send.at[k], s2_recv.at[k], far_at(k)).wait_recv()
-        tables(src)
+    def tables(b):
+        for k in range(1, near):
+            hand_on(b, k, near_id(near - k)).wait_recv()
+        for slot in range(*batches[b]):
+            both = zh * 0
+            t = far_id(slots[slot])
+            for bit in range(far.bit_length() - 1):
+                both = both + lax.rem(zh // (1 << bit), 2) * lax.rem(t // (1 << bit), 2)
+            far_sign = (1 - 2 * lax.rem(both, 2)).astype(jnp.float32)
+
+            @pl.loop(0, near)
+            def _(i):
+                place = samples[i, slot]
+                wide = [parity_sign(lane_bits & place)]
+                for bit in range(3, 7):
+                    factor = (1 - 2 * ((place >> bit) & 1)).astype(jnp.float32)
+                    wide = wide + [w * factor for w in wide]
+                had[slot, i] = jnp.concatenate(wide, axis=0).astype(jnp.bfloat16)
+                mask[slot, i] = parity_sign(high_bits & (place >> 7)) * far_sign
+
+    tables(0)
+    for b in (1, 2):
+        first, end = batches[b]
+        for slot in range(first, end):
+            sc_wait(slots[slot])
+        for k in range(1, near):
+            if end > first:
+                hand_on(b, k, g).start()
+    if batches[1][1] > batches[1][0]:
+        tables(1)
 
     for k in range(1, near):
         src = near_id(near - k)
@@ -171,28 +180,30 @@
     def pc(k):
         return copy(part_out.at[k], part_in.at[k], p_send.at[k], p_recv.at[k], far_at(k))
 
-    order = sorted(range(far), key=lambda k: -min(k, far - k))
-    for first, second in zip(order[::2], order[1::2]):
-        targets = (far_id(first), far_id(second))
-
-        @pl.loop(0, near)
-        def _(i):
-            table = jnp.concatenate([had[t, i] for t in targets], axis=1)
-            table = jnp.concatenate([table, table], axis=0)
-            product = jnp.dot(mixed[i], table, preferred_element_type=jnp.float32)
-            for n, (k, t) in enumerate(zip((first, second), targets)):
-                signs_t = mask[t, i]
-                total = None
-                for jh in range(groups):
-                    term = product[jh * block : (jh + 1) * block, n * LANES : (n + 1) * LANES] * signs_t[jh : jh + 1]
-                    total = term if jh == 0 else total + term
-                part_out[k, i] = total
-
-        for k in (first, second):
-            if k:
-                pc(k).start()
+    def partial_sums(order):
+        for pair in zip(order[::2], order[1::2]):
+            @pl.loop(0, near)
+            def _(i):
+                table = jnp.concatenate([had[slots.index(k), i] for k in pair], axis=1)
+                table = jnp.concatenate([table, table], axis=0)
+                product = jnp.dot(mixed[i], table, preferred_element_type=jnp.float32)
+                for n, k in enumerate(pair):
+                    signs_k = mask[slots.index(k), i]
+                    total = None
+                    for jh in range(groups):
+                        term = product[jh * block : (jh + 1) * block, n * LANES : (n + 1) * LANES] * signs_k[jh : jh + 1]
+                        total = term if jh == 0 else total + term
+                    part_out[k, i] = total
+
+            for k in pair:
+                if k:
+                    pc(k).start()
+
+    partial_sums(slots[1:close][::-1])
+    tables(2)
+    partial_sums(slots[close:][::-1] + [0])
     total = part_out[0]
-    for k in reversed([k for k in order if k]):
+    for k in slots[1:]:
         pc(k).wait_recv()
         total = total + part_in[k]
     own[g] = total * (1.0 / jnp.sqrt(jnp.float32(length * nx * nz)))
@@ -202,10 +213,11 @@
     def row_copy(k):
         return copy(own.at[g], rows.at[col], row_send.at[k], row_recv.at[k], col_at(k))
 
-    for k in range(1, cols):
-        row_copy(k).start()
-    for k in range(1, near):
-        own_copy(k).start()
+    for k in range(1, max(cols, near)):
+        if k < cols:
+            row_copy(k).start()
+        if k < near:
+            own_copy(k).start()
     rows[col] = own[g]
     for k in range(1, cols):
         src = col_id(cols - k)
@@ -242,9 +254,6 @@
         @pl.when(zh != nx * m + x)
         def _():
             tc(m).start()
-    for d in range(near):
-        sketch_ref[d * block : (d + 1) * block, :] = own[d, g]
-
     def fc(kx, kc):
         dest = lax.rem(x + kx, nx)
         return copy(
@@ -260,7 +269,7 @@
             total = total + tile_in[src]
         final[...] = total * (1.0 / (LANES * nx * nz))
         gathered[col] = final[x]
-        for kx in range(nx - 1, -1, -1):
+        for kx in range(nx):
             for kc in range(cols):
                 if kx or kc:
                     fc(kx, kc).start()
@@ -278,12 +287,17 @@
     for b in range(cols // 2):
         gram_ref[:, b * LANES : (b + 1) * LANES] = gathered[2 * b] + gathered[2 * b + 1]
 
-    for k in range(1, near):
-        s1(k).wait_send()
+    for d in range(near):
+        sketch_ref[d * block : (d + 1) * block, :] = own[d, g]
+
+    for k in range(1, near):
+        for b, (first, end) in enumerate(batches):
+            if end > first:
+                hand_on(b, k, g).wait_send()
         xc(k).wait_send()
         own_copy(k).wait_send()
     for k in range(1, far):
-        s2(k).wait_send()
+        sc(k).wait_send()
         pc(k).wait_send()
     for k in range(1, cols):
         row_copy(k).wait_send()
@@ -322,7 +336,7 @@
             vmem((1, LANES), i32),
             vmem((near, groups * block, LANES), f32),
             vmem((near, groups * block, LANES), f32),
-            vmem((far, near, 1, LANES), i32),
+            vmem((near, far, 1, LANES), i32),
             vmem((far, near, LANES, LANES), bf16),
             vmem((far, near, groups, LANES), f32),
             vmem((near, groups * block, 2 * LANES), bf16),
@@ -334,7 +348,7 @@
             vmem((far, nx, block, LANES), f32),
             vmem((nx, block, LANES), f32),
             vmem((cols, block, LANES), f32),
-            dma((3,)), dma((near,)), dma((near,)), dma((far,)), dma((far,)), dma((near,)), dma((near,)),
+            dma((3,)), dma((far,)), dma((far,)), dma((3, near)), dma((3, near)), dma((near,)), dma((near,)),
             dma((far,)), dma((far,)), dma((near,)), dma((near,)), dma((cols,)), dma((cols,)),
             dma((turns,)), dma((far,)), dma((nx, cols)), dma((cols,)),
         ],

time: 66.5 us -> 65.1 us (0.979)
  Pallas kernels: 63.7 us -> 62.2 us
    pallas_call x1, Pallas kernels: 63.7 us -> 62.2 us  [per_device(): pl.pallas_call(functools.partial(kernel, dims), out_shape=(jax.ShapeDtype...]
where the time goes in v3:
time: 65.1 us; the launch traced here: 64.8 us
  Pallas kernels  62.2 us (96%)
  local copies, waits for them, and re-layouts  1.99 us (3%)
    pallas_call x1, Pallas kernels, per_device(): pl.pallas_call(functools.partial(kernel, dims), out_shape=(jax.ShapeDtype...  62.2 us
    unnamed x4, local copies, waits for them, and re-layouts  1.99 us

profile of v3, /device:TPU:1, one launch (start us, length us, event | category | flops | bytes accessed | tf_op | source)
XLA Modules:
  0.0 64.8 jit_solution(8652144733830703838)
XLA Ops:
  0.6 62.2 %shard_map.50 = (f32[64,128]{1,0:T(8,128)}, f32[8,512]{1,0:T(8,128)}) custom-call(f32[64,2048]{1,0:T(8,128)} %panel_ref.1, s32[16,128]{1,0:T(8,128)} %bitcast.2, s32[1,128]{1,0:T(1,128)} %bitcast.3), custom_call_target="tpu_custom_call" | custom-call | flops 1073741824 | bytes 1048576 | tf_op jit(solution)/shard_map/pallas_call | solution.py:325
  62.8 0.0 copy-start
  62.9 1.4 %copy.7 = f32[64,128]{1,0:T(8,128)} copy(f32[64,128]{1,0:T(8,128)} %get-tuple-element.4) | data formatting | bytes 65536
  64.2 0.0 copy-done
  64.2 0.6 copy.8
Async XLA Ops:
  62.8 1.4 %copy-start = (f32[8,512]{1,0:T(8,128)S(1)}, f32[8,512]{1,0:T(8,128)}, u32[]{:S(2)}) copy-start(f32[8,512]{1,0:T(8,128)} %get-tuple-element.5) | copy-start | bytes 49156

commit v4 on v3

--- a/solution.py
+++ b/solution.py
@@ -38,9 +38,9 @@
 def kernel(
     dims, panel_ref, signs_ref, samp_ref, sketch_ref, gram_ref,
     panel, signs, samp, xs, xr, samples, had, mask, mixed, part_out, part_in,
-    own, rows, tile, tile_in, final, gathered,
+    own, rows, tile, tile_in, gathered, sketch, gram,
     load_sem, s_send, s_recv, pass_send, pass_recv, x_send, x_recv, p_send, p_recv,
-    own_send, own_recv, row_send, row_recv, t_send, t_recv, f_send, f_recv,
+    own_send, own_recv, row_send, row_recv, t_send, t_recv, f_send, f_recv, out_sem,
 ):
     nx, nz, ny, nc = dims
     width, length = panel.shape
@@ -147,7 +147,7 @@
                 both = both + lax.rem(zh // (1 << bit), 2) * lax.rem(t // (1 << bit), 2)
             far_sign = (1 - 2 * lax.rem(both, 2)).astype(jnp.float32)
 
-            @pl.loop(0, near)
+            @pl.loop(0, near, unroll=True)
             def _(i):
                 place = samples[i, slot]
                 wide = [parity_sign(lane_bits & place)]
@@ -182,7 +182,7 @@
 
     def partial_sums(order):
         for pair in zip(order[::2], order[1::2]):
-            @pl.loop(0, near)
+            @pl.loop(0, near, unroll=True)
             def _(i):
                 table = jnp.concatenate([had[slots.index(k), i] for k in pair], axis=1)
                 table = jnp.concatenate([table, table], axis=0)
@@ -244,51 +244,56 @@
         total = term if b == 0 else total + term
     tile[...] = total.reshape(tile.shape)
 
-    def tc(m):
-        target = nx * m + x
-        return copy(
-            tile.at[m], tile_in.at[zh], t_send.at[m], t_recv.at[zh], {"row": x * nz + 2 * target + zl, "col": col}
-        )
-
-    for m in range(turns):
-        @pl.when(zh != nx * m + x)
-        def _():
-            tc(m).start()
-    def fc(kx, kc):
-        dest = lax.rem(x + kx, nx)
-        return copy(
-            final.at[dest], gathered.at[col], f_send.at[kx, kc], f_recv.at[col], {"row": dest * nz + z, "col": col_id(kc)}
-        )
+    def mine(m, d):
+        return jnp.logical_and(zh == nx * m + x, x == d)
+
+    def tc(m, d):
+        where = {"row": d * nz + 2 * (nx * m + x) + zl, "col": col}
+        return copy(tile.at[m, d], tile_in.at[zh], t_send.at[m, d], t_recv.at[zh], where)
+
+    def each_tile(act):
+        for m in range(turns):
+            for d in range(nx):
+                @pl.when(jnp.logical_not(mine(m, d)))
+                def _():
+                    act(tc(m, d))
+
+    each_tile(lambda c: c.start())
 
     @pl.when(x == hub)
     def _():
-        total = tile[zh // nx]
-        for k in range(1, far):
-            src = far_id(far - k)
-            copy(tile.at[0], tile_in.at[src], t_send.at[0], t_recv.at[src], far_at(k)).wait_recv()
-            total = total + tile_in[src]
-        final[...] = total * (1.0 / (LANES * nx * nz))
-        gathered[col] = final[x]
-        for kx in range(nx):
-            for kc in range(cols):
-                if kx or kc:
-                    fc(kx, kc).start()
-    def incoming(k):
-        src = col_id(k)
-        return copy(final.at[0], gathered.at[src], f_send.at[0, k], f_recv.at[src], col_at(k))
-
-    for k in range(1, cols):
-        incoming(k).wait_recv()
+        tile_in[zh] = tile[zh // nx, x]
+
+    for d in range(near):
+        sketch[d * block : (d + 1) * block, :] = own[d, g]
+    outs = [pltpu.make_async_copy(sketch, sketch_ref, out_sem.at[0]), pltpu.make_async_copy(gram, gram_ref, out_sem.at[1])]
+    outs[0].start()
+
+    def tile_wait(k):
+        src = far_id(k)
+        copy(tile.at[0, 0], tile_in.at[src], t_send.at[0, 0], t_recv.at[src], far_at(1)).wait_recv()
 
     @pl.when(x != hub)
     def _():
-        copy(final.at[0], gathered.at[col], f_send.at[0, 1], f_recv.at[col], col_at(1)).wait_recv()
-
+        tile_wait(0)
+
+    total = tile_in[zh]
+    for k in slots[1:]:
+        tile_wait(k)
+        total = total + tile_in[far_id(k)]
+    gathered[col] = total * (1.0 / (LANES * nx * nz))
+
+    def fc(k):
+        return copy(gathered.at[col], gathered.at[col], f_send.at[k], f_recv.at[k], col_at(k))
+
+    for k in range(1, cols):
+        fc(k).start()
+    for k in range(1, cols):
+        there = gathered.at[col_id(cols - k)]
+        copy(there, there, f_send.at[k], f_recv.at[k], col_at(k)).wait_recv()
     for b in range(cols // 2):
-        gram_ref[:, b * LANES : (b + 1) * LANES] = gathered[2 * b] + gathered[2 * b + 1]
-
-    for d in range(near):
-        sketch_ref[d * block : (d + 1) * block, :] = own[d, g]
+        gram[:, b * LANES : (b + 1) * LANES] = gathered[2 * b] + gathered[2 * b + 1]
+    outs[1].start()
 
     for k in range(1, near):
         for b, (first, end) in enumerate(batches):
@@ -301,17 +306,10 @@
         pc(k).wait_send()
     for k in range(1, cols):
         row_copy(k).wait_send()
-    for m in range(turns):
-        @pl.when(zh != nx * m + x)
-        def _():
-            tc(m).wait_send()
-
-    @pl.when(x == hub)
-    def _():
-        for kx in range(nx):
-            for kc in range(cols):
-                if kx or kc:
-                    fc(kx, kc).wait_send()
+        fc(k).wait_send()
+    each_tile(lambda c: c.wait_send())
+    for c in outs:
+        c.wait()
 
 
 def per_device(dims, panel, signs, sample_rows):
@@ -329,7 +327,7 @@
             jax.ShapeDtypeStruct((block, width * cols), f32),
         ),
         in_specs=[pl.BlockSpec(memory_space=pl.ANY)] * 3,
-        out_specs=(pl.BlockSpec(memory_space=vmem), pl.BlockSpec(memory_space=vmem)),
+        out_specs=(pl.BlockSpec(memory_space=pl.ANY), pl.BlockSpec(memory_space=pl.ANY)),
         scratch_shapes=[
             vmem((width, length), f32),
             vmem((groups, LANES), i32),
@@ -345,12 +343,13 @@
             vmem((near, near, block, LANES), f32),
             vmem((cols, near, block, LANES), f32),
             vmem((turns, nx, block, LANES), f32),
-            vmem((far, nx, block, LANES), f32),
-            vmem((nx, block, LANES), f32),
+            vmem((far, block, LANES), f32),
             vmem((cols, block, LANES), f32),
+            vmem((width, LANES), f32),
+            vmem((block, width * cols), f32),
             dma((3,)), dma((far,)), dma((far,)), dma((3, near)), dma((3, near)), dma((near,)), dma((near,)),
             dma((far,)), dma((far,)), dma((near,)), dma((near,)), dma((cols,)), dma((cols,)),
-            dma((turns,)), dma((far,)), dma((nx, cols)), dma((cols,)),
+            dma((turns, nx)), dma((far,)), dma((cols,)), dma((cols,)), dma((2,)),
         ],
         compiler_params=pltpu.CompilerParams(
             collective_id=0, has_side_effects=True, vmem_limit_bytes=60 * 1024 * 1024

time: 65.1 us -> 63.4 us (0.974)
  Pallas kernels: 62.2 us -> 60.6 us
    pallas_call x1, Pallas kernels: 62.2 us -> 60.6 us  [per_device(): pl.pallas_call(functools.partial(kernel, dims), out_shape=(jax.ShapeDtype...]
where the time goes in v4:
time: 63.4 us; the launch traced here: 63.2 us
  Pallas kernels  60.6 us (96%)
  local copies, waits for them, and re-layouts  1.99 us (3%)
  between operations  0.65 us (1%)
    pallas_call x1, Pallas kernels, per_device(): pl.pallas_call(functools.partial(kernel, dims), out_shape=(jax.ShapeDtype...  60.6 us
    unnamed x4, local copies, waits for them, and re-layouts  1.99 us

profile of v4, /device:TPU:1, one launch (start us, length us, event | category | flops | bytes accessed | tf_op | source)
XLA Modules:
  0.0 63.2 jit_solution(3089380904966211767)
XLA Ops:
  0.6 60.6 %shard_map.50 = (f32[64,128]{1,0:T(8,128)}, f32[8,512]{1,0:T(8,128)}) custom-call(f32[64,2048]{1,0:T(8,128)} %panel_ref.1, s32[16,128]{1,0:T(8,128)} %bitcast.2, s32[1,128]{1,0:T(1,128)} %bitcast.3), custom_call_target="tpu_custom_call" | custom-call | flops 1073741824 | bytes 1048576 | tf_op jit(solution)/shard_map/pallas_call | solution.py:323
  61.2 0.0 copy-start
  61.2 1.4 %copy.7 = f32[64,128]{1,0:T(8,128)} copy(f32[64,128]{1,0:T(8,128)} %get-tuple-element.4) | data formatting | bytes 65536
  62.6 0.0 copy-done
  62.6 0.6 copy.8
Async XLA Ops:
  61.2 1.4 %copy-start = (f32[8,512]{1,0:T(8,128)S(1)}, f32[8,512]{1,0:T(8,128)}, u32[]{:S(2)}) copy-start(f32[8,512]{1,0:T(8,128)} %get-tuple-element.5) | copy-start | bytes 49156

commit v5 on v4

--- a/solution.py
+++ b/solution.py
@@ -81,8 +81,7 @@
     hub = lax.rem(zh, nx)
 
     slots = sorted(range(far), key=lambda k: (min(k, far - k), k))
-    close = 1 + sum(0 < min(k, far - k) <= far // 4 for k in slots)
-    batches = [(0, 1), (1, close), (close, far)]
+    batches = [(0, 1), (1, far)]
 
     loads = [
         pltpu.make_async_copy(src, dst, load_sem.at[i])
@@ -158,15 +157,10 @@
                 mask[slot, i] = parity_sign(high_bits & (place >> 7)) * far_sign
 
     tables(0)
-    for b in (1, 2):
-        first, end = batches[b]
-        for slot in range(first, end):
-            sc_wait(slots[slot])
-        for k in range(1, near):
-            if end > first:
-                hand_on(b, k, g).start()
-    if batches[1][1] > batches[1][0]:
-        tables(1)
+    for k in slots[1:]:
+        sc_wait(k)
+    for k in range(1, near):
+        hand_on(1, k, g).start()
 
     for k in range(1, near):
         src = near_id(near - k)
@@ -199,9 +193,8 @@
                 if k:
                     pc(k).start()
 
-    partial_sums(slots[1:close][::-1])
-    tables(2)
-    partial_sums(slots[close:][::-1] + [0])
+    tables(1)
+    partial_sums(slots[::-1])
     total = part_out[0]
     for k in slots[1:]:
         pc(k).wait_recv()
@@ -296,9 +289,8 @@
     outs[1].start()
 
     for k in range(1, near):
-        for b, (first, end) in enumerate(batches):
-            if end > first:
-                hand_on(b, k, g).wait_send()
+        for b in range(2):
+            hand_on(b, k, g).wait_send()
         xc(k).wait_send()
         own_copy(k).wait_send()
     for k in range(1, far):
@@ -347,7 +339,7 @@
             vmem((cols, block, LANES), f32),
             vmem((width, LANES), f32),
             vmem((block, width * cols), f32),
-            dma((3,)), dma((far,)), dma((far,)), dma((3, near)), dma((3, near)), dma((near,)), dma((near,)),
+            dma((3,)), dma((far,)), dma((far,)), dma((2, near)), dma((2, near)), dma((near,)), dma((near,)),
             dma((far,)), dma((far,)), dma((near,)), dma((near,)), dma((cols,)), dma((cols,)),
             dma((turns, nx)), dma((far,)), dma((cols,)), dma((cols,)), dma((2,)),
         ],

time: 63.4 us -> 61.7 us (0.973)
  Pallas kernels: 60.6 us -> 58.8 us
    pallas_call x1, Pallas kernels: 60.6 us -> 58.8 us  [per_device(): pl.pallas_call(functools.partial(kernel, dims), out_shape=(jax.ShapeDtype...]
where the time goes in v5:
time: 61.7 us; the launch traced here: 61.5 us
  Pallas kernels  58.8 us (95%)
  local copies, waits for them, and re-layouts  1.99 us (3%)
  between operations  0.65 us (1%)
    pallas_call x1, Pallas kernels, per_device(): pl.pallas_call(functools.partial(kernel, dims), out_shape=(jax.ShapeDtype...  58.8 us
    unnamed x4, local copies, waits for them, and re-layouts  1.99 us

profile of v5, /device:TPU:1, one launch (start us, length us, event | category | flops | bytes accessed | tf_op | source)
XLA Modules:
  0.0 61.5 jit_solution(18210936983018260601)
XLA Ops:
  0.6 58.8 %shard_map.50 = (f32[64,128]{1,0:T(8,128)}, f32[8,512]{1,0:T(8,128)}) custom-call(f32[64,2048]{1,0:T(8,128)} %panel_ref.1, s32[16,128]{1,0:T(8,128)} %bitcast.2, s32[1,128]{1,0:T(1,128)} %bitcast.3), custom_call_target="tpu_custom_call" | custom-call | flops 1073741824 | bytes 1048576 | tf_op jit(solution)/shard_map/pallas_call | solution.py:315
  59.5 0.0 copy-start
  59.5 1.4 %copy.7 = f32[64,128]{1,0:T(8,128)} copy(f32[64,128]{1,0:T(8,128)} %get-tuple-element.4) | data formatting | bytes 65536
  60.8 0.0 copy-done
  60.9 0.6 copy.8
Async XLA Ops:
  59.5 1.4 %copy-start = (f32[8,512]{1,0:T(8,128)S(1)}, f32[8,512]{1,0:T(8,128)}, u32[]{:S(2)}) copy-start(f32[8,512]{1,0:T(8,128)} %get-tuple-element.5) | copy-start | bytes 49156

commit v6 on v5

--- a/solution.py
+++ b/solution.py
@@ -136,26 +136,28 @@
     lane_bits = lax.broadcasted_iota(jnp.int32, (8, LANES), 0)
     high_bits = lax.broadcasted_iota(jnp.int32, (groups, LANES), 0)
 
-    def tables(b):
+    def passed_on(b):
         for k in range(1, near):
             hand_on(b, k, near_id(near - k)).wait_recv()
-        for slot in range(*batches[b]):
-            both = zh * 0
-            t = far_id(slots[slot])
-            for bit in range(far.bit_length() - 1):
-                both = both + lax.rem(zh // (1 << bit), 2) * lax.rem(t // (1 << bit), 2)
-            far_sign = (1 - 2 * lax.rem(both, 2)).astype(jnp.float32)
-
-            @pl.loop(0, near, unroll=True)
-            def _(i):
-                place = samples[i, slot]
-                wide = [parity_sign(lane_bits & place)]
-                for bit in range(3, 7):
-                    factor = (1 - 2 * ((place >> bit) & 1)).astype(jnp.float32)
-                    wide = wide + [w * factor for w in wide]
-                had[slot, i] = jnp.concatenate(wide, axis=0).astype(jnp.bfloat16)
-                mask[slot, i] = parity_sign(high_bits & (place >> 7)) * far_sign
-
+
+    def tables(slot):
+        both = zh * 0
+        t = far_id(slots[slot])
+        for bit in range(far.bit_length() - 1):
+            both = both + lax.rem(zh // (1 << bit), 2) * lax.rem(t // (1 << bit), 2)
+        far_sign = (1 - 2 * lax.rem(both, 2)).astype(jnp.float32)
+
+        @pl.loop(0, near, unroll=True)
+        def _(i):
+            place = samples[i, slot]
+            wide = [parity_sign(lane_bits & place)]
+            for bit in range(3, 7):
+                factor = (1 - 2 * ((place >> bit) & 1)).astype(jnp.float32)
+                wide = wide + [w * factor for w in wide]
+            had[slot, i] = jnp.concatenate(wide, axis=0).astype(jnp.bfloat16)
+            mask[slot, i] = parity_sign(high_bits & (place >> 7)) * far_sign
+
+    passed_on(0)
     tables(0)
     for k in slots[1:]:
         sc_wait(k)
@@ -176,6 +178,10 @@
 
     def partial_sums(order):
         for pair in zip(order[::2], order[1::2]):
+            for k in pair:
+                if k:
+                    tables(slots.index(k))
+
             @pl.loop(0, near, unroll=True)
             def _(i):
                 table = jnp.concatenate([had[slots.index(k), i] for k in pair], axis=1)
@@ -193,7 +199,7 @@
                 if k:
                     pc(k).start()
 
-    tables(1)
+    passed_on(1)
     partial_sums(slots[::-1])
     total = part_out[0]
     for k in slots[1:]:

time: 61.7 us -> 61.4 us (level)
  no operation moved by 1% of the time
where the time goes in v6:
time: 61.4 us; the launch traced here: 61.2 us
  Pallas kernels  58.5 us (95%)
  local copies, waits for them, and re-layouts  1.99 us (3%)
  between operations  0.65 us (1%)
    pallas_call x1, Pallas kernels, per_device(): pl.pallas_call(functools.partial(kernel, dims), out_shape=(jax.ShapeDtype...  58.5 us
    unnamed x4, local copies, waits for them, and re-layouts  1.99 us

profile of v6, /device:TPU:1, one launch (start us, length us, event | category | flops | bytes accessed | tf_op | source)
XLA Modules:
  0.0 61.2 jit_solution(4109796618468551393)
XLA Ops:
  0.6 58.5 %shard_map.50 = (f32[64,128]{1,0:T(8,128)}, f32[8,512]{1,0:T(8,128)}) custom-call(f32[64,2048]{1,0:T(8,128)} %panel_ref.1, s32[16,128]{1,0:T(8,128)} %bitcast.2, s32[1,128]{1,0:T(1,128)} %bitcast.3), custom_call_target="tpu_custom_call" | custom-call | flops 1073741824 | bytes 1048576 | tf_op jit(solution)/shard_map/pallas_call | solution.py:321
  59.2 0.0 copy-start
  59.2 1.4 %copy.7 = f32[64,128]{1,0:T(8,128)} copy(f32[64,128]{1,0:T(8,128)} %get-tuple-element.4) | data formatting | bytes 65536
  60.6 0.0 copy-done
  60.6 0.6 copy.8
Async XLA Ops:
  59.2 1.4 %copy-start = (f32[8,512]{1,0:T(8,128)S(1)}, f32[8,512]{1,0:T(8,128)}, u32[]{:S(2)}) copy-start(f32[8,512]{1,0:T(8,128)} %get-tuple-element.5) | copy-start | bytes 49156

commit v7 on v6

--- a/solution.py
+++ b/solution.py
@@ -268,32 +268,6 @@
     outs = [pltpu.make_async_copy(sketch, sketch_ref, out_sem.at[0]), pltpu.make_async_copy(gram, gram_ref, out_sem.at[1])]
     outs[0].start()
 
-    def tile_wait(k):
-        src = far_id(k)
-        copy(tile.at[0, 0], tile_in.at[src], t_send.at[0, 0], t_recv.at[src], far_at(1)).wait_recv()
-
-    @pl.when(x != hub)
-    def _():
-        tile_wait(0)
-
-    total = tile_in[zh]
-    for k in slots[1:]:
-        tile_wait(k)
-        total = total + tile_in[far_id(k)]
-    gathered[col] = total * (1.0 / (LANES * nx * nz))
-
-    def fc(k):
-        return copy(gathered.at[col], gathered.at[col], f_send.at[k], f_recv.at[k], col_at(k))
-
-    for k in range(1, cols):
-        fc(k).start()
-    for k in range(1, cols):
-        there = gathered.at[col_id(cols - k)]
-        copy(there, there, f_send.at[k], f_recv.at[k], col_at(k)).wait_recv()
-    for b in range(cols // 2):
-        gram[:, b * LANES : (b + 1) * LANES] = gathered[2 * b] + gathered[2 * b + 1]
-    outs[1].start()
-
     for k in range(1, near):
         for b in range(2):
             hand_on(b, k, g).wait_send()
@@ -304,6 +278,34 @@
         pc(k).wait_send()
     for k in range(1, cols):
         row_copy(k).wait_send()
+
+    def tile_wait(k):
+        src = far_id(k)
+        copy(tile.at[0, 0], tile_in.at[src], t_send.at[0, 0], t_recv.at[src], far_at(1)).wait_recv()
+
+    @pl.when(x != hub)
+    def _():
+        tile_wait(0)
+
+    total = tile_in[zh]
+    for k in slots[1:]:
+        tile_wait(k)
+        total = total + tile_in[far_id(k)]
+    gathered[col] = total * (1.0 / (LANES * nx * nz))
+
+    def fc(k):
+        return copy(gathered.at[col], gathered.at[col], f_send.at[k], f_recv.at[k], col_at(k))
+
+    for k in range(1, cols):
+        fc(k).start()
+    for k in range(1, cols):
+        there = gathered.at[col_id(cols - k)]
+        copy(there, there, f_send.at[k], f_recv.at[k], col_at(k)).wait_recv()
+    for b in range(cols // 2):
+        gram[:, b * LANES : (b + 1) * LANES] = gathered[2 * b] + gathered[2 * b + 1]
+    outs[1].start()
+
+    for k in range(1, cols):
         fc(k).wait_send()
     each_tile(lambda c: c.wait_send())
     for c in outs:

time: 61.4 us -> 61.4 us (level)
  no operation moved by 1% of the time
where the time goes in v7:
time: 61.4 us; the launch traced here: 61.2 us
  Pallas kernels  58.5 us (95%)
  local copies, waits for them, and re-layouts  1.99 us (3%)
  between operations  0.65 us (1%)
    pallas_call x1, Pallas kernels, per_device(): pl.pallas_call(functools.partial(kernel, dims), out_shape=(jax.ShapeDtype...  58.5 us
    unnamed x4, local copies, waits for them, and re-layouts  1.99 us

profile of v7, /device:TPU:1, one launch (start us, length us, event | category | flops | bytes accessed | tf_op | source)
XLA Modules:
  0.0 61.2 jit_solution(17668791822057085055)
XLA Ops:
  0.6 58.5 %shard_map.50 = (f32[64,128]{1,0:T(8,128)}, f32[8,512]{1,0:T(8,128)}) custom-call(f32[64,2048]{1,0:T(8,128)} %panel_ref.1, s32[16,128]{1,0:T(8,128)} %bitcast.2, s32[1,128]{1,0:T(1,128)} %bitcast.3), custom_call_target="tpu_custom_call" | custom-call | flops 1073741824 | bytes 1048576 | tf_op jit(solution)/shard_map/pallas_call | solution.py:323
  59.2 0.0 copy-start
  59.2 1.4 %copy.7 = f32[64,128]{1,0:T(8,128)} copy(f32[64,128]{1,0:T(8,128)} %get-tuple-element.4) | data formatting | bytes 65536
  60.6 0.0 copy-done
  60.6 0.6 copy.8
Async XLA Ops:
  59.2 1.4 %copy-start = (f32[8,512]{1,0:T(8,128)S(1)}, f32[8,512]{1,0:T(8,128)}, u32[]{:S(2)}) copy-start(f32[8,512]{1,0:T(8,128)} %get-tuple-element.5) | copy-start | bytes 49156
